TPU v7x, 512 devices: a whole 4x8x8 slice. The times are simulated.
512 devices in a mesh: streams: 16 (over y, core), tp: 32 (over x, z).
Axes of the slice: x: 4, y: 8, z: 8, core: 2. Of those that a mesh axis runs over, the one named last changes fastest.
Arguments:
- hidden_in: bfloat16 [512, 4, 1024], P(('streams', 'tp')), may hold values from -6 to 6
- byte_qkv: bfloat16 [512, 4, 1536], P(('streams', 'tp'))
- byte_cache: bfloat16 [512, 256, 512], P(('streams', 'tp'))
- byte_len: int32 [512], P(('streams', 'tp')), may hold values from 2 to 256, as said below
- flags: int32 [512, 4], P(('streams', 'tp')), may hold values 0 or 1
- coarse_prev: bfloat16 [512, 1024], P(('streams', 'tp')), may hold values from -6 to 6
- owner_map: int32 [32, 16, 1], replicated, may hold values from 0 to 15; in each aligned block of 16 rows (0 to 15, 16 to 31, ..., all dimensions but the last counted through in order) at most 2 rows name the same one
- up_weight: bfloat16 [1024, 8192], P(None, 'tp'), may hold values from -0.1875 to 0.1875
- coarse_gain: float32 [8192], replicated, may hold values from 0.5 to 1.5
- query_weight: bfloat16 [8192, 4096], P(None, 'tp'), may hold values from -0.0625 to 0.0625
- keyval_weight: bfloat16 [8192, 1024], P('tp'), may hold values from -0.0625 to 0.0625
- return_weight: bfloat16 [4096, 1024], P('tp'), may hold values from -0.09375 to 0.09375
- coarse_cache: bfloat16 [16, 64, 32, 32, 256], P('streams', None, 'tp'), as said below
- coarse_len: int32 [16, 64], P('streams'), may hold values from 1 to 32, as said below
Outputs:
- byte_out: bfloat16 [512, 4, 1024], P(('streams', 'tp'))
Inputs may be any that keep to these rules, and one draw needn't show every extreme that they name: `owner_map`: within one index c of tp, no group owns more than 2 of the sequences s * 32 + c, and some group owns exactly 2. `byte_len`: some sequence has exactly 256 filled positions. `coarse_len`: some slot has exactly 32 filled positions. `coarse_cache`: the copies for heads h and h2 are equal where h // 8 = h2 // 8.
All inputs are finite; a program needn't handle non-finite values. No bound on the sum of `flags` on one device may be relied on, other than what follows from the above.
Results may differ from a plain program's by a relative error of at most 0.014.
Values may be sent and summed in bfloat16 or wider, within the bound.
A program may use at most 64 MiB of HBM per device.

v0:
```python
import jax
import jax.numpy as jnp
from jax import lax
from jax.sharding import PartitionSpec as P

HD = 128
OWNED_MOST = 2
EPSILON = 1e-05
NEG_FILL = -1e30


def split_softmax(scores_old, scores_new):
    largest = jnp.maximum(
        jnp.max(scores_old, axis=-1, keepdims=True), jnp.max(scores_new, axis=-1, keepdims=True)
    )
    exp_old = jnp.exp(scores_old - largest)
    exp_new = jnp.exp(scores_new - largest)
    denominator = jnp.sum(exp_old, axis=-1, keepdims=True) + jnp.sum(
        exp_new, axis=-1, keepdims=True
    )
    return (
        (exp_old / denominator).astype(jnp.bfloat16),
        (exp_new / denominator).astype(jnp.bfloat16),
    )


def rank_table(owner_map):
    owners = owner_map[:, :, 0]
    group_total = owners.shape[1]
    same_owner = owners[:, :, None] == owners[:, None, :]
    earlier = (
        jnp.arange(group_total, dtype=jnp.int32)[None, :, None]
        > jnp.arange(group_total, dtype=jnp.int32)[None, None, :]
    )
    ranking = jnp.sum((same_owner & earlier).astype(jnp.int32), axis=2)
    return (owners, ranking)


def byte_attention(byte_qkv, byte_cache, byte_len):
    number, step_count, total_width = byte_qkv.shape
    length = byte_cache.shape[1]
    kv_width = byte_cache.shape[2] // 2
    kv_groups = kv_width // HD
    head_count = (total_width - 2 * kv_width) // HD
    group_size = head_count // kv_groups
    query_part = byte_qkv[:, :, : head_count * HD].reshape(
        number, step_count, kv_groups, group_size, HD
    )
    new_keys = byte_qkv[:, :, head_count * HD : head_count * HD + kv_width].reshape(
        number, step_count, kv_groups, HD
    )
    new_values = byte_qkv[:, :, head_count * HD + kv_width :].reshape(
        number, step_count, kv_groups, HD
    )
    old_keys = byte_cache[:, :, :kv_width].reshape(number, length, kv_groups, HD)
    old_values = byte_cache[:, :, kv_width:].reshape(number, length, kv_groups, HD)
    scaling = HD ** (-0.5)
    scores_old = (
        jnp.einsum("nsgjd,nlgd->nsgjl", query_part, old_keys, preferred_element_type=jnp.float32)
        * scaling
    )
    valid_old = jnp.arange(length, dtype=jnp.int32)[None, :] < byte_len[:, None]
    scores_old = jnp.where(valid_old[:, None, None, None, :], scores_old, NEG_FILL)
    scores_new = (
        jnp.einsum("nsgjd,nugd->nsgju", query_part, new_keys, preferred_element_type=jnp.float32)
        * scaling
    )
    causal = jnp.arange(step_count)[:, None] >= jnp.arange(step_count)[None, :]
    scores_new = jnp.where(causal[None, :, None, None, :], scores_new, NEG_FILL)
    weights_old, weights_new = split_softmax(scores_old, scores_new)
    mixed_heads = jnp.einsum(
        "nsgjl,nlgd->nsgjd", weights_old, old_values, preferred_element_type=jnp.float32
    )
    mixed_heads = mixed_heads + jnp.einsum(
        "nsgju,nugd->nsgjd", weights_new, new_values, preferred_element_type=jnp.float32
    )
    return mixed_heads.reshape(number, step_count, head_count * HD)


def dispatch(block_rows, block_marks, owners, ranking):
    column_total = lax.axis_size("tp")
    row_index = lax.axis_index("streams")
    every_rows, every_marks = (
        lax.all_gather(block_rows, ("streams", "tp"), axis=0, tiled=True),
        lax.all_gather(block_marks, ("streams", "tp"), axis=0, tiled=True),
    )
    target = jnp.where(
        owners == row_index,
        jnp.arange(column_total, dtype=jnp.int32)[:, None] * OWNED_MOST + ranking,
        -1,
    )
    target_flat = target.T.reshape(-1)
    slot_ids = jnp.arange(column_total * OWNED_MOST, dtype=jnp.int32)
    picker = (slot_ids[:, None] == target_flat[None, :]).astype(jnp.bfloat16)
    slot_rows = jnp.einsum(
        "ai,ibd->abd", picker, every_rows, preferred_element_type=jnp.float32
    ).astype(jnp.bfloat16)
    slot_marks = jnp.einsum("ai,ib->ab", picker, every_marks, preferred_element_type=jnp.float32)
    return (slot_rows, slot_marks)


def coarse_project(slot_rows, up_weight, coarse_gain, query_weight, keyval_weight):
    column_total = lax.axis_size("tp")
    column = lax.axis_index("tp")
    part_width = up_weight.shape[1]
    expanded = jnp.einsum(
        "rbd,df->rbf", slot_rows, up_weight, preferred_element_type=jnp.float32
    ).astype(jnp.bfloat16)
    widened = lax.all_gather(expanded, "tp", axis=2, tiled=True).astype(jnp.float32)
    scaled_part = (widened * coarse_gain).astype(jnp.bfloat16)
    query_sum = jnp.einsum(
        "rbf,fh->rbh", scaled_part, query_weight, preferred_element_type=jnp.float32
    )
    squares = jnp.sum(widened * widened, axis=2)
    query_sum, squares = (query_sum, squares)
    own_gains = lax.dynamic_slice_in_dim(coarse_gain, column * part_width, part_width, 0)
    own_scaled = (expanded.astype(jnp.float32) * own_gains).astype(jnp.bfloat16)
    inverse = lax.rsqrt(squares / (part_width * column_total) + EPSILON)[:, :, None]
    queries = (query_sum * inverse).astype(jnp.bfloat16)
    kv_width = keyval_weight.shape[1]
    kv_heads = kv_width // (2 * HD)
    group_size = column_total // kv_heads
    head_group = column // group_size
    keyval_part = jnp.einsum(
        "rbf,fc->rbc", own_scaled, keyval_weight, preferred_element_type=jnp.float32
    )
    keyvals = lax.psum(keyval_part, "tp")
    new_keys = (lax.dynamic_slice_in_dim(keyvals, head_group * HD, HD, 2) * inverse).astype(
        jnp.bfloat16
    )
    new_values = (
        lax.dynamic_slice_in_dim(keyvals, (kv_heads + head_group) * HD, HD, 2) * inverse
    ).astype(jnp.bfloat16)
    return (queries, new_keys, new_values)


def coarse_attention(queries, step_ids, cache_own, cache_len, key_store, value_store, mark_store):
    length = cache_own.shape[1]
    step_count = key_store.shape[1]
    scaling = HD ** (-0.5)
    scores_old = (
        jnp.einsum(
            "rbd,rld->rbl", queries, cache_own[:, :, :HD], preferred_element_type=jnp.float32
        )
        * scaling
    )
    valid_old = jnp.arange(length, dtype=jnp.int32)[None, :] < cache_len[:, None]
    scores_old = jnp.where(valid_old[:, None, :], scores_old, NEG_FILL)
    scores_new = (
        jnp.einsum("rbd,rud->rbu", queries, key_store, preferred_element_type=jnp.float32) * scaling
    )
    valid_new = (jnp.arange(step_count)[None, None, :] <= step_ids[None, :, None]) & (
        mark_store[:, None, :] > 0.5
    )
    scores_new = jnp.where(valid_new, scores_new, NEG_FILL)
    weights_old, weights_new = split_softmax(scores_old, scores_new)
    mixed_heads = jnp.einsum(
        "rbl,rld->rbd", weights_old, cache_own[:, :, HD:], preferred_element_type=jnp.float32
    )
    mixed_heads = mixed_heads + jnp.einsum(
        "rbu,rud->rbd", weights_new, value_store, preferred_element_type=jnp.float32
    )
    return mixed_heads.astype(jnp.bfloat16)


def give_back(mixed_heads, return_weight, owners, ranking):
    row_index = lax.axis_index("streams")
    column = lax.axis_index("tp")
    summed = lax.psum_scatter(
        jnp.einsum("rbh,hd->rbd", mixed_heads, return_weight, preferred_element_type=jnp.float32),
        "tp",
        scatter_dimension=0,
        tiled=True,
    ).astype(jnp.bfloat16)
    every_back = lax.all_gather(summed, "streams", axis=0, tiled=True)
    my_owner = lax.dynamic_index_in_dim(
        lax.dynamic_index_in_dim(owners, column, 0, keepdims=False), row_index, 0, keepdims=False
    )
    my_rank = lax.dynamic_index_in_dim(
        lax.dynamic_index_in_dim(ranking, column, 0, keepdims=False), row_index, 0, keepdims=False
    )
    return lax.dynamic_index_in_dim(every_back, my_owner * OWNED_MOST + my_rank, 0, keepdims=False)


def shards(
    hidden_in,
    byte_qkv,
    byte_cache,
    byte_len,
    flags,
    coarse_prev,
    owner_map,
    up_weight,
    coarse_gain,
    query_weight,
    keyval_weight,
    return_weight,
    coarse_cache,
    coarse_len,
):
    step_count = hidden_in.shape[1]
    attended = byte_attention(byte_qkv, byte_cache, byte_len)
    byte_rows = (hidden_in.astype(jnp.float32) + attended).astype(jnp.bfloat16)
    byte_marks = flags.astype(jnp.bfloat16)
    owners, ranking = rank_table(owner_map)
    cache_own = coarse_cache[0, :, 0]
    cache_len = coarse_len[0]
    slot_rows, slot_marks = dispatch(byte_rows, byte_marks, owners, ranking)
    queries, new_keys, new_values = coarse_project(
        slot_rows, up_weight, coarse_gain, query_weight, keyval_weight
    )
    step_ids = jnp.arange(step_count, dtype=jnp.int32)
    mixed_heads = coarse_attention(
        queries, step_ids, cache_own, cache_len, new_keys, new_values, slot_marks
    )
    given_back = give_back(mixed_heads, return_weight, owners, ranking)
    current = coarse_prev[0].astype(jnp.float32)
    outputs = []
    for step in range(step_count):
        current = jnp.where(flags[0, step] > 0, given_back[step].astype(jnp.float32), current)
        outputs.append(byte_rows[0, step].astype(jnp.float32) + current)
    return jnp.stack(outputs)[None].astype(jnp.bfloat16)


def solution(mesh):
    return jax.shard_map(
        shards,
        mesh=mesh,
        in_specs=(
            P(("streams", "tp"), None, None),
            P(("streams", "tp"), None, None),
            P(("streams", "tp"), None, None),
            P(("streams", "tp")),
            P(("streams", "tp"), None),
            P(("streams", "tp"), None),
            P(),
            P(None, "tp"),
            P(),
            P(None, "tp"),
            P("tp", None),
            P("tp", None),
            P("streams", None, "tp", None, None),
            P("streams", None),
        ),
        out_specs=P(("streams", "tp"), None, None),
        check_vma=False,
    )
```

profile of v0, /device:TPU:1, one launch (start us, length us, event | category | flops | bytes accessed | tf_op | source)
XLA Modules:
  0.0 587.4 jit_solution(7376833832583837293)
XLA Ops:
  6.6 1.1 fusion.96
  7.9 0.7 slice.62
  9.3 0.9 convolution_multiply_fusion.2
  10.2 0.2 fusion.98
  10.9 0.2 fusion.58
  11.1 0.9 fusion.32
  12.0 0.7 fusion.61
  12.7 0.6 copy.147
  13.4 0.9 convert_reduce_fusion
  14.3 0.7 select_bitcast_fusion
  15.1 122.9 %all-gather.4.cloned.1.call-done = bf16[512,4,1024]{2,1,0:T(4,128)(2,1)} async-done(((bf16[1,4,1024]{2,1,0:T(4,128)(2,1)}), bf16[512,4,1024]{2,1,0:T(4,128)(2,1)}) %all-gather.4.cloned.1.call-update) | async-done | bytes 4194320 | tf_op jit(solution)/shard_map/all_gather | solution.py:84
  138.0 5.7 fusion.14
  143.8 1.2 fusion.100
  145.1 0.6 dynamic_slice.27
  146.9 90.5 %all-gather = bf16[512,1,4]{2,1,0:T(2,128)(2,1)S(1)} all-gather(bf16[1,1,4]{2,1,0:T(2,128)(2,1)S(1)} %convert_bitcast_fusion), channel_id=1, replica_groups=mesh['streams'=16,'tp'=32] {'streams','tp'}, dimensions={0}, use_global_device_ids=true | all-gather | bytes 4104 | tf_op jit(solution)/shard_map/all_gather | solution.py:85
  237.6 0.7 fusion.97
  240.9 1.3 dynamic-slice.4
  243.1 2.2 fusion.35
  245.4 3.3 fusion.1
  248.8 1.2 fusion.23
  250.1 148.3 %all-reduce.4.cloned.1.call-done = f32[64,4,1024]{2,0,1:T(8,128)} async-done(((f32[64,4,1024]{2,0,1:T(8,128)}), f32[64,4,1024]{2,0,1:T(8,128)}) %all-reduce.4.cloned.1.call-update) | async-done | bytes 1048592 | tf_op jit(solution)/shard_map/psum | solution.py:127
  398.4 1.1 multiply_convert_fusion.2
  399.5 0.2 fusion.48
  400.0 1.5 fusion.99
  401.6 0.2 fusion.44
  402.5 1.4 fusion.28
  403.9 0.3 fusion.38
  404.2 0.7 copy.161
  404.9 125.0 %all-reduce.5 = bf16[64,4,1024]{2,1,0:T(4,128)(2,1)} all-reduce(f32[64,4,1024]{2,1,0:T(4,128)S(1)} %copy.161), channel_id=2, replica_groups=mesh['streams'=16,'tp'=32] {'tp'}, use_global_device_ids=true, to_apply=%region_11.12.clone | all-reduce | flops 262144 | bytes 1572864
  529.9 0.7 dynamic-slice_convert_fusion
  530.6 49.6 %all_gather.15 = bf16[32,4,1024]{2,1,0:T(4,128)(2,1)S(1)} all-gather(bf16[2,4,1024]{2,1,0:T(4,128)(2,1)S(1)} %dynamic-slice_convert_fusion), channel_id=1, replica_groups=mesh['streams'=16,'tp'=32] {'streams'}, dimensions={0}, use_global_device_ids=true | all-gather | bytes 278528 | tf_op jit(solution)/shard_map/all_gather | solution.py:175
  580.2 0.6 pad_maximum_fusion
  (59 shorter events, 2.7 us)
Async XLA Ops:
  6.5 242.1 %copy-start = (bf16[8192,128]{1,0:T(8,128)(2,1)S(1)}, bf16[8192,128]{1,0:T(8,128)(2,1)}, u32[]{:S(2)}) copy-start(bf16[8192,128]{1,0:T(8,128)(2,1)} %param.23) | copy-start | bytes 6291460
  6.5 140.4 %copy-start.4 = (s32[1,4]{1,0:T(1,128)S(1)}, s32[1,4]{1,0:T(1,128)}, u32[]{:S(2)}) copy-start(s32[1,4]{1,0:T(1,128)} %param.18) | copy-start | bytes 52
  6.5 131.5 %all-gather.4.cloned.1.call-start = ((), (), s32[]{:S(2)}) async-start(), calls=%async_computation | async-start | bytes 4202496 | tf_op jit(solution)/shard_map/all_gather | solution.py:84
  6.5 234.3 %copy-start.7 = (f32[8192]{0:T(1024)S(1)}, f32[8192]{0:T(1024)}, u32[]{:S(2)}) copy-start(f32[8192]{0:T(1024)} %param.22) | copy-start | bytes 98308
  6.6 236.4 %copy-start.6 = (s32[1,64]{1,0:T(1,128)S(1)}, s32[1,64]{1,0:T(1,128)}, u32[]{:S(2)}) copy-start(s32[1,64]{1,0:T(1,128)} %param.27) | copy-start | bytes 772
  6.6 236.5 %copy-start.2 = (bf16[256,1024]{1,0:T(8,128)(2,1)S(1)}, bf16[256,1024]{1,0:T(8,128)(2,1)}, u32[]{:S(2)}) copy-start(bf16[256,1024]{1,0:T(8,128)(2,1)} %param.24) | copy-start | bytes 1572868
  13.3 232.0 %all-gather.6.cloned.1.call-start = ((), (), s32[]{:S(2)}) async-start(), calls=%async_computation.1 | async-start | bytes 4325376 | tf_op jit(solution)/shard_map/all_gather | solution.py:109
  143.7 254.7 %all-reduce.4.cloned.1.call-start = ((), (), s32[]{:S(2)}) async-start(), calls=%async_computation.2 | async-start | bytes 2097152 | tf_op jit(solution)/shard_map/psum | solution.py:127
  245.4 3.5 copy-start.1
  250.1 153.9 %copy-start.3 = (bf16[128,1024]{1,0:T(8,128)(2,1)S(1)}, bf16[128,1024]{1,0:T(8,128)(2,1)}, u32[]{:S(2)}) copy-start(bf16[128,1024]{1,0:T(8,128)(2,1)} %param.25) | copy-start | bytes 786436
  401.5 178.7 %copy-start.5 = (bf16[1,1024]{1,0:T(2,128)(2,1)S(1)}, bf16[1,1024]{1,0:T(2,128)(2,1)}, u32[]{:S(2)}) copy-start(bf16[1,1024]{1,0:T(2,128)(2,1)} %param.19) | copy-start | bytes 6148
Sparse Core Ops, SparseCore 0:
  13.5 124.5 all-gather.3
  143.8 85.0 all-gather.5
  245.4 152.8 all-reduce.3
where the time goes:
time: 588 us; the launch traced here: 587 us
  waiting for transfers between devices  271 us (46%)
  blocking collectives  265 us (45%)
  between operations  18.6 us (3%)
  matrix products  15 us (3%)
  other arithmetic  9.66 us (2%)
  local copies, waits for them, and re-layouts  7.67 us (1%)
    psum x1, waiting for transfers between devices, coarse_project(): keyvals = lax.psum(keyval_part, 'tp')  148 us
    unnamed x1, blocking collectives  125 us
    all_gather x1, waiting for transfers between devices, dispatch(): lax.all_gather(block_rows, ('streams', 'tp'), axis=0, tiled=True)  123 us
    all_gather x1, blocking collectives, dispatch(): lax.all_gather(block_marks, ('streams', 'tp'), axis=0, tiled=True)  90.5 us
    all_gather x1, blocking collectives, give_back(): every_back = lax.all_gather(summed, 'streams', axis=0, tiled=True)  49.6 us
  transfers between devices with their start and end apart: 3, of which 2 were waited for; matrix products, arithmetic and copies ran while one was open for 2% of the time, Pallas kernels for 0%

commit v1 on v0

--- a/solution.py
+++ b/solution.py
@@ -124,7 +124,9 @@
     keyval_part = jnp.einsum(
         "rbf,fc->rbc", own_scaled, keyval_weight, preferred_element_type=jnp.float32
     )
-    keyvals = lax.psum(keyval_part, "tp")
+    keyvals = keyval_part
+    for hop in (1, 2, 4, 8, 16):
+        keyvals = keyvals + lax.ppermute(keyvals, "tp", [(dev, dev ^ hop) for dev in range(32)])
     new_keys = (lax.dynamic_slice_in_dim(keyvals, head_group * HD, HD, 2) * inverse).astype(
         jnp.bfloat16
     )

time: 588 us -> 619 us (1.053)
  starting transfers between devices: 0.09 us -> 17.4 us
  waiting for transfers between devices: 271 us -> 280 us
    ppermute x0 -> x5, waiting for transfers between devices: none -> 157 us  [coarse_project(): lax.ppermute(keyvals, 'tp', [(dev, dev ^ hop) for dev in range(32)])]
    psum x1 -> x0, waiting for transfers between devices: 148 us -> none  [coarse_project(): keyvals = lax.psum(keyval_part, 'tp')]
    ppermute x0 -> x5, starting transfers between devices: none -> 17.3 us  [coarse_project(): lax.ppermute(keyvals, 'tp', [(dev, dev ^ hop) for dev in range(32)])]
    all_gather x1, blocking collectives: 90.5 us -> 101 us  [dispatch(): lax.all_gather(block_marks, ('streams', 'tp'), axis=0, tiled=True)]
    all_gather x1, blocking collectives: 49.6 us -> 43.2 us  [give_back(): every_back = lax.all_gather(summed, 'streams', axis=0, tiled=True)]
  transfers between devices with their start and end apart: 3 -> 7, of which waited for: 2 -> 5; matrix products, arithmetic and copies ran while one was open for 2% -> 2% of each run, Pallas kernels for 0% -> 0%
where the time goes in v1:
time: 619 us; the launch traced here: 618 us
  waiting for transfers between devices  280 us (45%)
  blocking collectives  268 us (43%)
  between operations  19 us (3%)
  starting transfers between devices  17.4 us (3%)
  matrix products  14 us (2%)
  other arithmetic  12.7 us (2%)
  local copies, waits for them, and re-layouts  7.53 us (1%)
    ppermute x5, waiting for transfers between devices, coarse_project(): lax.ppermute(keyvals, 'tp', [(dev, dev ^ hop) for dev in range(32)])  157 us
    unnamed x1, blocking collectives  123 us
    all_gather x1, waiting for transfers between devices, dispatch(): lax.all_gather(block_rows, ('streams', 'tp'), axis=0, tiled=True)  123 us
    all_gather x1, blocking collectives, dispatch(): lax.all_gather(block_marks, ('streams', 'tp'), axis=0, tiled=True)  101 us
    all_gather x1, blocking collectives, give_back(): every_back = lax.all_gather(summed, 'streams', axis=0, tiled=True)  43.2 us
    ppermute x5, starting transfers between devices, coarse_project(): lax.ppermute(keyvals, 'tp', [(dev, dev ^ hop) for dev in range(32)])  17.3 us
  transfers between devices with their start and end apart: 7, of which 5 were waited for; matrix products, arithmetic and copies ran while one was open for 2% of the time, Pallas kernels for 0%

profile of v1, /device:TPU:1, one launch (start us, length us, event | category | flops | bytes accessed | tf_op | source)
XLA Modules:
  0.0 618.2 jit_solution(16436530492811540680)
XLA Ops:
  6.6 1.1 fusion.96
  7.9 0.7 slice.62
  9.3 0.9 convolution_multiply_fusion.2
  11.1 0.9 fusion.32
  12.0 0.7 fusion.61
  13.4 0.9 convert_reduce_fusion
  14.3 0.7 select_bitcast_fusion
  15.1 122.9 %all-gather.4.cloned.1.call-done = bf16[512,4,1024]{2,1,0:T(4,128)(2,1)} async-done(((bf16[1,4,1024]{2,1,0:T(4,128)(2,1)}), bf16[512,4,1024]{2,1,0:T(4,128)(2,1)}) %all-gather.4.cloned.1.call-update) | async-done | bytes 4194320 | tf_op jit(solution)/shard_map/all_gather | solution.py:84
  138.0 5.7 fusion.14
  143.8 1.2 fusion.35
  145.0 2.5 collective-permute-start
  147.5 26.9 %collective-permute-done = f32[64,4,1024]{2,0,1:T(8,128)S(1)} collective-permute-done((f32[64,4,1024]{2,0,1:T(8,128)S(1)}, f32[64,4,1024]{2,0,1:T(8,128)S(1)}, u32[]{:S(2)}, u32[]{:S(2)}) %collective-permute-start) | collective-permute-done | bytes 1048608 | tf_op jit(solution)/shard_map/ppermute | solution.py:129
  174.6 2.4 collective-permute-start.1
  177.0 48.2 %collective-permute-done.1 = f32[64,4,1024]{2,0,1:T(8,128)S(1)} collective-permute-done((f32[64,4,1024]{2,0,1:T(8,128)S(1)}, f32[64,4,1024]{2,0,1:T(8,128)S(1)}, u32[]{:S(2)}, u32[]{:S(2)}) %collective-permute-start.1) | collective-permute-done | bytes 1048608 | tf_op jit(solution)/shard_map/ppermute | solution.py:129
  225.4 5.6 collective-permute-start.2
  231.1 59.6 %collective-permute-done.2 = f32[64,4,1024]{2,0,1:T(8,128)S(1)} collective-permute-done((f32[64,4,1024]{2,0,1:T(8,128)S(1)}, f32[64,4,1024]{2,0,1:T(8,128)S(1)}, u32[]{:S(2)}, u32[]{:S(2)}) %collective-permute-start.2) | collective-permute-done | bytes 1048608 | tf_op jit(solution)/shard_map/ppermute | solution.py:129
  290.8 1.9 collective-permute-start.3
  292.8 22.0 %collective-permute-done.3 = f32[64,4,1024]{2,0,1:T(8,128)S(1)} collective-permute-done((f32[64,4,1024]{2,0,1:T(8,128)S(1)}, f32[64,4,1024]{2,0,1:T(8,128)S(1)}, u32[]{:S(2)}, u32[]{:S(2)}) %collective-permute-start.3) | collective-permute-done | bytes 1048608 | tf_op jit(solution)/shard_map/ppermute | solution.py:129
  314.9 5.0 collective-permute-start.4
  319.9 1.2 fusion.100
  323.1 101.1 %all-gather = bf16[512,1,4]{2,1,0:T(2,128)(2,1)S(1)} all-gather(bf16[1,1,4]{2,1,0:T(2,128)(2,1)S(1)} %convert_bitcast_fusion), channel_id=1, replica_groups=mesh['streams'=16,'tp'=32] {'streams','tp'}, dimensions={0}, use_global_device_ids=true | all-gather | bytes 4104 | tf_op jit(solution)/shard_map/all_gather | solution.py:85
  427.6 1.3 dynamic-slice.4
  429.8 2.4 add.132
  432.2 3.3 fusion.1
  435.4 1.1 multiply_convert_fusion.2
  436.5 1.2 fusion.23
  438.3 1.5 fusion.99
  440.9 1.4 fusion.28
  442.6 0.7 copy.161
  443.2 123.5 %all-reduce.2 = bf16[64,4,1024]{2,1,0:T(4,128)(2,1)} all-reduce(f32[64,4,1024]{2,1,0:T(4,128)S(1)} %copy.161), channel_id=2, replica_groups=mesh['streams'=16,'tp'=32] {'tp'}, use_global_device_ids=true, to_apply=%region_10.11.clone | all-reduce | flops 262144 | bytes 1572864
  566.7 0.7 dynamic-slice_convert_fusion
  567.4 43.2 %all_gather.15 = bf16[32,4,1024]{2,1,0:T(4,128)(2,1)S(1)} all-gather(bf16[2,4,1024]{2,1,0:T(4,128)(2,1)S(1)} %dynamic-slice_convert_fusion), channel_id=1, replica_groups=mesh['streams'=16,'tp'=32] {'streams'}, dimensions={0}, use_global_device_ids=true | all-gather | bytes 278528 | tf_op jit(solution)/shard_map/all_gather | solution.py:177
  (71 shorter events, 6.8 us)
Async XLA Ops:
  6.5 430.0 %copy-start = (bf16[8192,128]{1,0:T(8,128)(2,1)S(1)}, bf16[8192,128]{1,0:T(8,128)(2,1)}, u32[]{:S(2)}) copy-start(bf16[8192,128]{1,0:T(8,128)(2,1)} %param.23) | copy-start | bytes 6291460
  6.5 137.2 %copy-start.7 = (f32[8192]{0:T(1024)S(1)}, f32[8192]{0:T(1024)}, u32[]{:S(2)}) copy-start(f32[8192]{0:T(1024)} %param.22) | copy-start | bytes 98308
  6.5 137.2 %copy-start.2 = (bf16[256,1024]{1,0:T(8,128)(2,1)S(1)}, bf16[256,1024]{1,0:T(8,128)(2,1)}, u32[]{:S(2)}) copy-start(bf16[256,1024]{1,0:T(8,128)(2,1)} %param.24) | copy-start | bytes 1572868
  6.5 131.5 %all-gather.4.cloned.1.call-start = ((), (), s32[]{:S(2)}) async-start(), calls=%async_computation | async-start | bytes 4202496 | tf_op jit(solution)/shard_map/all_gather | solution.py:84
  13.3 418.9 %all-gather.6.cloned.1.call-start = ((), (), s32[]{:S(2)}) async-start(), calls=%async_computation.1 | async-start | bytes 4325376 | tf_op jit(solution)/shard_map/all_gather | solution.py:109
  145.0 29.4 %collective-permute-start = (f32[64,4,1024]{2,0,1:T(8,128)S(1)}, f32[64,4,1024]{2,0,1:T(8,128)S(1)}, u32[]{:S(2)}, u32[]{:S(2)}) collective-permute-start(f32[64,4,1024]{2,0,1:T(8,128)S(1)} %fusion.35), channel_id=1, source_target_pairs={{0,1},{1,0},{2,3},{3,2},{4,5},{5,4},{6,7},{7,6},{8,9},{9,8},{10,11... | collective-permute-start | bytes 3145736 | tf_op jit(solution)/shard_map/ppermute | solution.py:129
  174.6 148.4 %copy-start.4 = (s32[1,4]{1,0:T(1,128)S(1)}, s32[1,4]{1,0:T(1,128)}, u32[]{:S(2)}) copy-start(s32[1,4]{1,0:T(1,128)} %param.18) | copy-start | bytes 52
  174.6 50.6 %collective-permute-start.1 = (f32[64,4,1024]{2,0,1:T(8,128)S(1)}, f32[64,4,1024]{2,0,1:T(8,128)S(1)}, u32[]{:S(2)}, u32[]{:S(2)}) collective-permute-start(f32[64,4,1024]{2,0,1:T(8,128)S(1)} %add.128), channel_id=1, source_target_pairs={{0,2},{1,3},{2,0},{3,1},{4,6},{5,7},{6,4},{7,5},{8,10},{9,11},{10,... | collective-permute-start | bytes 3145736 | tf_op jit(solution)/shard_map/ppermute | solution.py:129
  225.4 204.2 %copy-start.6 = (s32[1,64]{1,0:T(1,128)S(1)}, s32[1,64]{1,0:T(1,128)}, u32[]{:S(2)}) copy-start(s32[1,64]{1,0:T(1,128)} %param.27) | copy-start | bytes 772
  225.4 65.2 %collective-permute-start.2 = (f32[64,4,1024]{2,0,1:T(8,128)S(1)}, f32[64,4,1024]{2,0,1:T(8,128)S(1)}, u32[]{:S(2)}, u32[]{:S(2)}) collective-permute-start(f32[64,4,1024]{2,0,1:T(8,128)S(1)} %add.129), channel_id=1, source_target_pairs={{0,4},{1,5},{2,6},{3,7},{4,0},{5,1},{6,2},{7,3},{8,12},{9,13},{10,... | collective-permute-start | bytes 3145736 | tf_op jit(solution)/shard_map/ppermute | solution.py:129
  290.8 23.9 %collective-permute-start.3 = (f32[64,4,1024]{2,0,1:T(8,128)S(1)}, f32[64,4,1024]{2,0,1:T(8,128)S(1)}, u32[]{:S(2)}, u32[]{:S(2)}) collective-permute-start(f32[64,4,1024]{2,0,1:T(8,128)S(1)} %add.130), channel_id=1, source_target_pairs={{0,8},{1,9},{2,10},{3,11},{4,12},{5,13},{6,14},{7,15},{8,0},{9,1},... | collective-permute-start | bytes 3145736 | tf_op jit(solution)/shard_map/ppermute | solution.py:129
  314.9 114.8 %collective-permute-start.4 = (f32[64,4,1024]{2,0,1:T(8,128)S(1)}, f32[64,4,1024]{2,0,1:T(8,128)}, u32[]{:S(2)}, u32[]{:S(2)}) collective-permute-start(f32[64,4,1024]{2,0,1:T(8,128)S(1)} %add.131), channel_id=1, source_target_pairs={{0,16},{1,17},{2,18},{3,19},{4,20},{5,21},{6,22},{7,23},{8,24},{9,... | collective-permute-start | bytes 3145736 | tf_op jit(solution)/shard_map/ppermute | solution.py:129
  432.2 4.4 copy-start.1
  436.5 5.7 copy-start.3
  439.8 170.9 %copy-start.5 = (bf16[1,1024]{1,0:T(2,128)(2,1)S(1)}, bf16[1,1024]{1,0:T(2,128)(2,1)}, u32[]{:S(2)}) copy-start(bf16[1,1024]{1,0:T(2,128)(2,1)} %param.19) | copy-start | bytes 6148
Sparse Core Ops, SparseCore 0:
  13.4 124.5 all-gather.3
  143.8 161.3 all-gather.5
